TPU v7x, 256 devices: a whole 4x4x8 slice. The times are simulated.
256 devices in a mesh: row: 8 (over x, z_lo), col: 32 (over y, z_hi, core).
Axes of the slice: x: 4, y: 4, z: 8 (z_hi: 4, z_lo: 2; z = z_hi * 2 + z_lo), core: 2. Of those that a mesh axis runs over, the one named last changes fastest.
Arguments:
- query_grads: bfloat16 [1024, 28672], P('col', 'row'), may hold values from -6 to 6
- query_inputs: bfloat16 [1024, 8192], P(None, 'col'), may hold values from -6 to 6
- out_basis: bfloat16 [28672, 28672], P('row', 'col'), may hold values from -0.03125 to 0.03125
- in_basis: bfloat16 [8192, 8192], P('col', 'row'), may hold values from -0.0625 to 0.0625
- eig_grid: bfloat16 [28672, 8192], P('col', 'row'), may hold values from 0.0019989014 to 0.19921875
Outputs:
- scaled: bfloat16 [28672, 8192], P('col', 'row')
All inputs are finite; a program needn't handle non-finite values.
Results may differ from a plain program's by a relative error of at most 0.0058.
Values may be sent and summed in bfloat16 or wider, within the bound.
A program may use at most 64 MiB of HBM per device.

v0:
```python
import jax
import jax.numpy as jnp
from jax import lax
from jax.sharding import PartitionSpec as P

damping = 0.01


def shards(query_grads, query_inputs, out_basis, in_basis, eig_grid):
    partial_value = jnp.dot(
        lax.all_gather(query_grads, "col", axis=0, tiled=True),
        out_basis,
        preferred_element_type=jnp.float32,
    )
    rotated_out = lax.psum(partial_value, "row").astype(jnp.bfloat16)
    in_partial = jnp.dot(query_inputs, in_basis, preferred_element_type=jnp.float32)
    rotated_in = lax.psum(in_partial, "col").astype(jnp.bfloat16)
    coeffs = lax.dot_general(
        rotated_out, rotated_in, (((0,), (0,)), ((), ())), preferred_element_type=jnp.float32
    )
    total = rotated_out.shape[0]
    scaled = coeffs / total / (eig_grid.astype(jnp.float32) + damping)
    return scaled.astype(jnp.bfloat16)


def solution(mesh):
    return jax.shard_map(
        shards,
        mesh=mesh,
        in_specs=(
            P("col", "row"),
            P(None, "col"),
            P("row", "col"),
            P("col", "row"),
            P("col", "row"),
        ),
        out_specs=P("col", "row"),
        check_vma=False,
    )
```

profile of v0, /device:TPU:2, one launch (start us, length us, event | category | flops | bytes accessed | tf_op | source)
XLA Modules:
  0.0 389.0 jit_solution(16574025154335470380)
XLA Ops:
  6.5 0.0 copy-start
  6.5 0.0 all-gather.2.cloned.1.call-start
  6.5 0.7 all-gather.2.cloned.1.call-update
  7.3 0.3 copy-done
  7.6 3.8 fusion.8
  11.4 211.0 %all-reduce.3 = bf16[1024,1024]{1,0:T(8,128)(2,1)S(1)} all-reduce(f32[1024,1024]{1,0:T(8,128)} %fusion.8), channel_id=1, replica_groups=mesh['row'=8,'col'=32] {'col'}, use_global_device_ids=true, to_apply=%region_1.0 | all-reduce | flops 1048576 | bytes 6291456 | tf_op jit(solution)/shard_map/psum | solution.py:17
  222.4 0.0 all-gather.2.cloned.1.call-done
  222.5 13.1 %fusion.7 = f32[1024,896]{1,0:T(8,128)} fusion(bf16[1024,3584]{1,0:T(8,128)(2,1)} %all-gather.2.cloned.1.call-done, bf16[3584,896]{1,0:T(8,128)(2,1)} %param.7), kind=kOutput, calls=%fused_computation.4 | convolution fusion | flops 6576668672 | bytes 17432576 | tf_op jit(solution)/shard_map/dot_general | solution.py:10
  235.6 140.9 %all-reduce.2 = bf16[1024,896]{1,0:T(8,128)(2,1)} all-reduce(f32[1024,896]{1,0:T(8,128)} %fusion.7), channel_id=1, replica_groups=mesh['row'=8,'col'=32] {'row'}, use_global_device_ids=true, to_apply=%region_0.0 | all-reduce | flops 917504 | bytes 5505024 | tf_op jit(solution)/shard_map/psum | solution.py:15
  376.5 5.7 %divide_convert_fusion = bf16[896,1024]{1,0:T(8,128)(2,1)} fusion(bf16[896,1024]{1,0:T(8,128)(2,1)} %param.9, bf16[1024,1024]{1,0:T(8,128)(2,1)S(1)} %all-reduce.3, bf16[1024,896]{1,0:T(8,128)(2,1)} %all-reduce.2), kind=kOutput, calls=%fused_computation | convolution fusion | flops 1883635712 | bytes 7602176 | tf_op jit(solution)/shard_map/dot_general | solution.py:18
Async XLA Ops:
  6.5 1.0 copy-start
  6.5 215.9 %all-gather.2.cloned.1.call-start = ((), (), s32[]{:S(2)}) async-start(), calls=%async_computation | async-start | bytes 7569408 | tf_op jit(solution)/shard_map/all_gather | solution.py:11
Sparse Core Ops, SparseCore 0:
  9.9 93.2 all-gather.1
where the time goes:
time: 389 us
  blocking collectives  352 us (90%)
  matrix products  22.6 us (6%)
  between operations  13.4 us (3%)
    psum x1, blocking collectives, shards(): rotated_in = lax.psum(in_partial, 'col').astype(jnp.bfloat16)  211 us
    psum x1, blocking collectives, shards(): rotated_out = lax.psum(partial_value, 'row').astype(jnp.bfloat16)  141 us
    dot_general x1, matrix products, shards(): jnp.dot(lax.all_gather(query_grads, 'col', axis=0, tiled=True), out_basis...  13.1 us
  transfers between devices with their start and end apart: 1, of which 0 were waited for; matrix products, arithmetic and copies ran while one was open for 1% of the time, Pallas kernels for 0%

commit v1 on v0

v1 whole, which is shorter than its diff:
```python
import jax
import jax.numpy as jnp
from jax import lax
from jax.experimental import pallas as pl
from jax.experimental.pallas import tpu as pltpu
from jax.sharding import PartitionSpec as P

damping = 0.01
MESH = pl.DeviceIdType.MESH
SLABS = (0, 1, 3, 2)
MAX_COPIES = 160


def kernel(g_in, q_in, bo_in, bi_in, eig_in, out, G, B, QI, IB, RIp, RIf, RZ, JYb, JYf, RY, RI,
           Pb, Pf, RX, SB, SZ, RO, ACC, EIG, OUT, ssem, rsem, lsem):
    f32, bf16 = jnp.float32, jnp.bfloat16
    r, c = lax.axis_index("row"), lax.axis_index("col")
    x, zl = r // 2, r % 2
    y, zh, k = c // 8, (c // 2) % 4, c % 2

    def dev(dx=0, dy=0, dz=0, flip_zl=False, flip_k=False):
        zl_to = 1 - zl if flip_zl else zl
        k_to = 1 - k if flip_k else k
        return ((x + dx) % 4 * 2 + zl_to, (y + dy) % 4 * 8 + (zh + dz) % 4 * 2 + k_to)

    sib = dev(flip_k=True)
    yp, ym, y2 = dev(dy=1), dev(dy=3), dev(dy=2)
    zp, zm, z2 = dev(dz=1), dev(dz=3), dev(dz=2)
    xp, xm, x2 = dev(dx=1), dev(dx=3), dev(dx=2)
    zlp = dev(flip_zl=True)
    partners = (sib, yp, ym, y2, zp, zm, z2, xp, xm, x2, zlp)

    loads = {}

    def load(name, src, dst):
        cp = pltpu.make_async_copy(src, dst, lsem.at[len(loads)])
        cp.start()
        loads[name] = cp

    load("q", q_in.at[:, :, k], QI.at[k])
    load("bi", bi_in, IB.at[k])
    load("g", g_in, G.at[0, 0, k])
    load("bo", bo_in, B)
    load("eig", eig_in, EIG)

    barrier = pltpu.get_barrier_semaphore()
    for p in partners:
        pl.semaphore_signal(barrier, inc=1, device_id=p, device_id_type=MESH)
    pl.semaphore_wait(barrier, len(partners))

    copies = {}

    def send(name, src, dst, to):
        n = len(copies)
        cp = pltpu.make_async_remote_copy(src_ref=src, dst_ref=dst, send_sem=ssem.at[n], recv_sem=rsem.at[n],
                                          device_id=to, device_id_type=MESH)
        cp.start()
        copies[name] = cp

    def got(name):
        copies[name].wait_recv()

    def gather_z(tag, buf, own):
        send(tag + "z3", own, buf.at[3, 0, k], zp)
        send(tag + "z1", own, buf.at[1, 0, k], zm)

    def gather_y(tag, buf, dz, own):
        send(tag + f"y3{dz}", own, buf.at[dz, 3, k], yp)
        send(tag + f"y1{dz}", own, buf.at[dz, 1, k], ym)
        send(tag + f"s0{dz}", own, buf.at[dz, 0, k], sib)

    lo, hi = pl.ds(0, 16), pl.ds(16, 16)

    def gather_z_arrive(tag, buf):
        got(tag + "z3")
        send(tag + "z2lo", buf.at[3, 0, k, lo], buf.at[2, 0, k, lo], zp)
        gather_y(tag, buf, 3, buf.at[3, 0, k])
        got(tag + "z1")
        send(tag + "z2hi", buf.at[1, 0, k, hi], buf.at[2, 0, k, hi], zm)
        gather_y(tag, buf, 1, buf.at[1, 0, k])

    def gather_z_arrive2(tag, buf):
        got(tag + "z2lo")
        got(tag + "z2hi")
        gather_y(tag, buf, 2, buf.at[2, 0, k])

    def gather_y_arrive(tag, buf, dz):
        got(tag + f"y3{dz}")
        send(tag + f"y2lo{dz}", buf.at[dz, 3, k, lo], buf.at[dz, 2, k, lo], yp)
        send(tag + f"s3{dz}", buf.at[dz, 3, k], buf.at[dz, 3, k], sib)
        got(tag + f"y1{dz}")
        send(tag + f"y2hi{dz}", buf.at[dz, 1, k, hi], buf.at[dz, 1 + 1, k, hi], ym)
        send(tag + f"s1{dz}", buf.at[dz, 1, k], buf.at[dz, 1, k], sib)

    def gather_y_arrive2(tag, buf, dz):
        got(tag + f"y2lo{dz}")
        got(tag + f"y2hi{dz}")
        send(tag + f"s2{dz}", buf.at[dz, 2, k], buf.at[dz, 2, k], sib)

    def gather_sib(tag, dz):
        for dy in range(4):
            got(tag + f"s{dy}{dz}")

    def in_start():
        send("bi", bi_in, IB.at[k], sib)
        send("q", q_in.at[:, :, 1 - k], QI.at[k], sib)

    def in_partial():
        loads["q"].wait()
        loads["bi"].wait()
        got("bi")
        got("q")
        for yy in range(4):
            total = jnp.zeros((128, 1024), f32)
            for kf in range(2):
                total += jnp.dot(QI[kf, yy].reshape(128, 256), IB[kf], preferred_element_type=f32)
            total = total.reshape(4, 32, 1024)
            for zz in range(4):
                RIf[zz, yy] = total[zz]
                RIp[zz, yy] = total[zz].astype(bf16)

    def in_z_send():
        send("iz2", RIp.at[(zh + 2) % 4], RZ.at[0], z2)
        send("iz1", RIp.at[(zh + 1) % 4], RZ.at[1], zp)
        send("iz3", RIp.at[(zh + 3) % 4], RZ.at[2], zm)

    def in_y_send():
        for d in "213":
            got("iz" + d)
        total = RIf[zh]
        for i in range(3):
            total += RZ[i].astype(f32)
        JYf[...] = total
        JYb[...] = total.astype(bf16)
        send("iy2", JYb.at[(y + 2) % 4], RY.at[0], y2)
        send("iy1", JYb.at[(y + 1) % 4], RY.at[1], yp)
        send("iy3", JYb.at[(y + 3) % 4], RY.at[2], ym)

    def in_final():
        for d in "213":
            got("iy" + d)
        total = JYf[y]
        for i in range(3):
            total += RY[i].astype(f32)
        RI[0, 0, k] = total.astype(bf16)
        gather_z("r", RI, RI.at[0, 0, k])
        gather_y("r", RI, 0, RI.at[0, 0, k])

    def out_partial(q):
        slab = G.at[q]
        for n0, n1 in ((0, 512), (512, 896)):
            part = jnp.dot(slab[...].reshape(256, 3584), B[:, n0:n1], preferred_element_type=f32)
            part = part.reshape(4, 2, 32, n1 - n0)
            Pf[q, :, :, :, n0:n1] = part
            Pb[q, :, :, :, n0:n1] = part.astype(bf16)
        send(f"x2{q}", Pb.at[q, (x + 2) % 4], RX.at[q, 0], x2)
        send(f"x1{q}", Pb.at[q, (x + 1) % 4], RX.at[q, 1], xp)
        send(f"x3{q}", Pb.at[q, (x + 3) % 4], RX.at[q, 2], xm)

    def out_x(q):
        for d in "213":
            got(f"x{d}{q}")
        total = Pf[q, x]
        for i in range(3):
            total += RX[q, i].astype(f32)
        Pf[q, x] = total
        SB[q] = Pf[q, x, 1 - zl].astype(bf16)
        send(f"zl{q}", SB.at[q], SZ.at[q], zlp)

    def out_zl(q):
        got(f"zl{q}")
        RO[q, x, zl] = (Pf[q, x, zl] + SZ[q].astype(f32)).astype(bf16)
        mine = RO.at[q, x, zl]
        send(f"oz{q}", mine, mine, zlp)
        send(f"op{q}", mine, mine, xp)
        send(f"om{q}", mine, mine, xm)

    def out_gather1(q):
        got(f"oz{q}")
        other = RO.at[q, x, 1 - zl]
        send(f"opz{q}", other, other, xp)
        send(f"omz{q}", other, other, xm)

    def out_gather2(q):
        for name in ("op", "om", "opz", "omz"):
            got(name + str(q))
        left, right = RO.at[q, (x + 3) % 4, 0], RO.at[q, (x + 1) % 4, 1]
        send(f"o2p{q}", left, left, xp)
        send(f"o2m{q}", right, right, xm)

    def coeffs(q, first):
        got(f"o2p{q}")
        got(f"o2m{q}")
        part = lax.dot_general(RO[q].reshape(256, 896), RI[q].reshape(256, 1024), (((0,), (0,)), ((), ())),
                               preferred_element_type=f32)
        if first:
            ACC[...] = part
        else:
            ACC[...] += part

    gather_z("g", G, g_in)
    gather_y("g", G, 0, g_in)
    in_start()
    in_partial()
    loads["g"].wait()
    gather_y_arrive("g", G, 0)
    gather_z_arrive("g", G)
    in_z_send()
    gather_y_arrive2("g", G, 0)
    gather_sib("g", 0)
    loads["bo"].wait()
    out_partial(0)
    gather_z_arrive2("g", G)
    gather_y_arrive("g", G, 1)
    gather_y_arrive("g", G, 3)
    out_x(0)
    gather_y_arrive2("g", G, 1)
    out_zl(0)
    gather_sib("g", 1)
    out_gather1(0)
    out_partial(1)
    out_gather2(0)
    gather_y_arrive("g", G, 2)
    gather_y_arrive2("g", G, 3)
    out_x(1)
    in_y_send()
    gather_sib("g", 3)
    out_zl(1)
    in_final()
    out_partial(3)
    out_gather1(1)
    gather_y_arrive2("g", G, 2)
    out_gather2(1)
    gather_z_arrive("r", RI)
    gather_sib("g", 2)
    out_partial(2)
    out_x(3)
    gather_y_arrive("r", RI, 0)
    gather_z_arrive2("r", RI)
    out_zl(3)
    gather_y_arrive("r", RI, 1)
    gather_y_arrive("r", RI, 3)
    out_x(2)
    out_gather1(3)
    gather_y_arrive("r", RI, 2)
    out_zl(2)
    gather_y_arrive2("r", RI, 0)
    gather_y_arrive2("r", RI, 1)
    out_gather2(3)
    out_gather1(2)
    gather_y_arrive2("r", RI, 3)
    gather_y_arrive2("r", RI, 2)
    gather_sib("r", 0)
    coeffs(0, True)
    out_gather2(2)
    gather_sib("r", 1)
    coeffs(1, False)
    gather_sib("r", 3)
    coeffs(3, False)
    gather_sib("r", 2)
    coeffs(2, False)
    loads["eig"].wait()
    outs = []
    for i in range(4):
        rows = pl.ds(i * 224, 224)
        OUT[rows] = (ACC[rows] / 1024 / (EIG[rows].astype(f32) + damping)).astype(bf16)
        cp = pltpu.make_async_copy(OUT.at[rows], out.at[rows], lsem.at[len(loads) + i])
        cp.start()
        outs.append(cp)
    for cp in copies.values():
        cp.wait_send()
    for cp in outs:
        cp.wait()


def shards(query_grads, query_inputs, out_basis, in_basis, eig_grid):
    bf16, f32, vmem = jnp.bfloat16, jnp.float32, pltpu.VMEM
    any_space = pl.BlockSpec(memory_space=pl.ANY)
    return pl.pallas_call(
        kernel,
        out_shape=jax.ShapeDtypeStruct((896, 1024), bf16),
        in_specs=[any_space] * 5,
        out_specs=any_space,
        scratch_shapes=[
            vmem((4, 4, 2, 32, 3584), bf16),
            vmem((3584, 896), bf16),
            vmem((2, 4, 4, 32, 256), bf16),
            vmem((2, 256, 1024), bf16),
            vmem((4, 4, 32, 1024), bf16),
            vmem((4, 4, 32, 1024), f32),
            vmem((3, 4, 32, 1024), bf16),
            vmem((4, 32, 1024), bf16),
            vmem((4, 32, 1024), f32),
            vmem((3, 32, 1024), bf16),
            vmem((4, 4, 2, 32, 1024), bf16),
            vmem((4, 4, 2, 32, 896), bf16),
            vmem((4, 4, 2, 32, 896), f32),
            vmem((4, 3, 2, 32, 896), bf16),
            vmem((4, 32, 896), bf16),
            vmem((4, 32, 896), bf16),
            vmem((4, 4, 2, 32, 896), bf16),
            vmem((896, 1024), f32),
            vmem((896, 1024), bf16),
            vmem((896, 1024), bf16),
            pltpu.SemaphoreType.DMA((MAX_COPIES,)),
            pltpu.SemaphoreType.DMA((MAX_COPIES,)),
            pltpu.SemaphoreType.DMA((9,)),
        ],
        compiler_params=pltpu.CompilerParams(
            collective_id=0, has_side_effects=True, vmem_limit_bytes=56 * 2**20
        ),
        cost_estimate=pl.CostEstimate(flops=9_000_000_000, bytes_accessed=12_000_000, transcendentals=0),
        name="precondition",
    )(query_grads, query_inputs.reshape(4, 4, 2, 32, 256), out_basis, in_basis, eig_grid)


def solution(mesh):
    return jax.shard_map(
        shards,
        mesh=mesh,
        in_specs=(
            P("col", "row"),
            P(None, "col"),
            P("row", "col"),
            P("col", "row"),
            P("col", "row"),
        ),
        out_specs=P("col", "row"),
        check_vma=False,
    )
```

time: 389 us -> 111 us (0.29)
  the two profiles are of different devices: /device:TPU:2 before, /device:TPU:32 now
where the time goes in v1:
time: 111 us
  Pallas kernels  108 us (97%)
  local copies, waits for them, and re-layouts  2.87 us (3%)
    pallas_call x1, Pallas kernels, shards(): pl.pallas_call(kernel, out_shape=jax.ShapeDtypeStruct((896, 1024), bf16),...  108 us
    unnamed x1, local copies, waits for them, and re-layouts  2.87 us

profile of v1, /device:TPU:32, one launch (start us, length us, event | category | flops | bytes accessed | tf_op | source)
XLA Modules:
  0.0 110.7 jit_solution(11837131474678297121)
XLA Ops:
  0.0 107.8 %precondition.1 = bf16[896,1024]{1,0:T(8,128)(2,1)} custom-call(bf16[32,3584]{1,0:T(8,128)(2,1)} %g_in.1, bf16[4,4,2,32,256]{4,3,2,1,0:T(8,128)(2,1)} %bitcast.1, bf16[3584,896]{1,0:T(8,128)(2,1)} %bo_in.1, bf16[256,1024]{1,0:T(8,128)(2,1)} %bi_in.1, bf16[896,1024]{1,0:T(8,128)(2,1)} %eig_in.1), custom_call_target="tpu_custom_call" | custom-call | flops 8999999488 | bytes 12000000 | tf_op jit(solution)/shard_map/precondition/pallas_call | solution.py:279
  107.8 2.9 %copy.7 = bf16[896,1024]{1,0:T(8,128)(2,1)} copy(bf16[896,1024]{1,0:T(8,128)(2,1)} %precondition.1) | data formatting | bytes 3670016

commit v2 on v0

v2 whole, which is shorter than its diff:
```python
import jax
import jax.numpy as jnp
from jax import lax
from jax.experimental import pallas as pl
from jax.experimental.pallas import tpu as pltpu
from jax.sharding import PartitionSpec as P

damping = 0.01
MESH = pl.DeviceIdType.MESH
SENT, ARRIVED = 12, 101


def kernel(g_in, q_in, bo_in, bi_in, eig_in, out, G, B, QI, IB, RIp, RIf, RZ, JYb, JYf, RY, RI,
           Pb, Pf, RX, SB, SZ, RO, ACC, EIG, OUT, ssem, rsem, lsem):
    f32, bf16 = jnp.float32, jnp.bfloat16
    r, c = lax.axis_index("row"), lax.axis_index("col")
    x, zl = r // 2, r % 2
    y, zh, k = c // 8, (c // 2) % 4, c % 2

    def dev(dx=0, dy=0, dz=0, flip_zl=False, flip_k=False):
        zl_to = 1 - zl if flip_zl else zl
        k_to = 1 - k if flip_k else k
        return ((x + dx) % 4 * 2 + zl_to, (y + dy) % 4 * 8 + (zh + dz) % 4 * 2 + k_to)

    sib = dev(flip_k=True)
    yp, ym, y2 = dev(dy=1), dev(dy=3), dev(dy=2)
    zp, zm, z2 = dev(dz=1), dev(dz=3), dev(dz=2)
    xp, xm, x2 = dev(dx=1), dev(dx=3), dev(dx=2)
    zlp = dev(flip_zl=True)
    partners = (sib, yp, ym, y2, zp, zm, z2, xp, xm, x2, zlp)

    loads = {}

    def load(name, src, dst):
        cp = pltpu.make_async_copy(src, dst, lsem.at[len(loads)])
        cp.start()
        loads[name] = cp

    load("q", q_in.at[:, :, k], QI.at[k])
    load("bi", bi_in, IB.at[k])
    load("g", g_in, G.at[0, 0, k])
    load("bo", bo_in, B)
    load("eig", eig_in, EIG)

    barrier = pltpu.get_barrier_semaphore()
    for p in partners:
        pl.semaphore_signal(barrier, inc=1, device_id=p, device_id_type=MESH)
    pl.semaphore_wait(barrier, len(partners))

    sent, arrived = {}, {}

    def copy(group, name, src, dst, to):
        out_sem = ssem.at[sent.setdefault(group, len(sent))]
        in_sem = rsem.at[arrived.setdefault(name, len(arrived))]
        return pltpu.make_async_remote_copy(src_ref=src, dst_ref=dst, send_sem=out_sem, recv_sem=in_sem,
                                            device_id=to, device_id_type=MESH)

    def send(group, name, src, dst, to):
        copy(group, name, src, dst, to).start()

    def got(name, ref):
        copy("ibi", name, ref, ref, sib).wait_recv()

    def all_sent(group, ref):
        copy(group, "ibi", ref, ref, sib).wait_send()

    def part(buf, q, h, dy):
        return buf.at[q, dy, k, pl.ds(16 * h, 16)]

    def send_y(t, buf, q, halves):
        for h in (0, 1):
            send(t + "y", f"{t}y3{q}{h}", halves[h], part(buf, q, h, 3), yp)
            send(t + "y", f"{t}y1{q}{1 - h}", halves[1 - h], part(buf, q, 1 - h, 1), ym)

    def gather_start(t, buf, own):
        halves = [own.at[pl.ds(16 * h, 16)] for h in range(2)]
        send(t + "z", t + "z1", halves[0], part(buf, 1, 0, 0), zp)
        send(t + "z", t + "z1", halves[1], part(buf, 1, 1, 0), zm)
        send(t + "z", t + "z2", halves[1], part(buf, 2, 1, 0), zp)
        send(t + "z", t + "z2", halves[0], part(buf, 2, 0, 0), zm)
        send_y(t, buf, 0, halves)
        send(t + "s", t + "s0", own, buf.at[0, 0, k], sib)

    def gather_z(t, buf, q):
        got(f"{t}z{q}", buf.at[q, 0, k])
        halves = [part(buf, q, h, 0) for h in range(2)]
        if q == 1:
            send(t + "z", t + "z3", halves[0], part(buf, 3, 0, 0), zp)
            send(t + "z", t + "z3", halves[1], part(buf, 3, 1, 0), zm)
        send_y(t, buf, q, halves)
        send(t + "s", f"{t}s{q}", buf.at[q, 0, k], buf.at[q, 0, k], sib)

    def gather_y(t, buf, dy, q, h):
        src = part(buf, q, h, dy)
        got(f"{t}y{dy}{q}{h}", src)
        if (dy, h) == (3, 0):
            send(t + "y", f"{t}y2{q}", src, part(buf, q, 0, 2), yp)
        if (dy, h) == (1, 1):
            send(t + "y", f"{t}y2{q}", src, part(buf, q, 1, 2), ym)
        send(t + "s", f"{t}s{q}", src, src, sib)

    def gather_far(t, buf, q):
        src = buf.at[q, 2, k]
        got(f"{t}y2{q}", src)
        send(t + "s", f"{t}s{q}", src, src, sib)

    def gather_done(t, buf, q):
        got(f"{t}s{q}", buf.at[q, :, 1 - k])

    def in_start():
        send("ibi", "ibi", bi_in, IB.at[k], sib)
        send("iq", "iq", q_in.at[:, :, 1 - k], QI.at[k], sib)

    def in_partial():
        loads["q"].wait()
        loads["bi"].wait()
        got("ibi", IB.at[1 - k])
        got("iq", QI.at[1 - k])
        for yy in range(4):
            total = jnp.zeros((128, 1024), f32)
            for kf in range(2):
                total += jnp.dot(QI[kf, yy].reshape(128, 256), IB[kf], preferred_element_type=f32)
            total = total.reshape(4, 32, 1024)
            for zz in range(4):
                RIf[zz, yy] = total[zz]
                RIp[zz, yy] = total[zz].astype(bf16)

    zn, zb, zo = (zh + 1) % 4, (zh + 3) % 4, (zh + 2) % 4
    lo, hi = pl.ds(0, 16), pl.ds(16, 16)

    def in_far(j):
        yj = (y + j) % 4
        send("i", f"iA+{j}", RIp.at[zo, yj, lo], RZ.at[0, j], zp)
        send("i", f"iA-{j}", RIp.at[zo, yj, hi], RZ.at[1, j], zm)

    def in_near(j):
        yj = (y + j) % 4
        send("i", f"iD{j}", RIp.at[zn, yj, hi], RZ.at[2, j], zp)
        send("i", f"iD{j}", RIp.at[zb, yj, lo], RZ.at[3, j], zm)

    def in_add(way, j):
        got(f"iA{way}{j}", RZ.at[0 if way == "+" else 1, j])
        yj = (y + j) % 4
        if way == "+":
            RIp[zn, yj, lo] = (RIf[zn, yj, lo] + RZ[0, j].astype(f32)).astype(bf16)
            send("i", f"iD{j}", RIp.at[zn, yj, lo], RZ.at[4, j], zp)
        else:
            RIp[zb, yj, hi] = (RIf[zb, yj, hi] + RZ[1, j].astype(f32)).astype(bf16)
            send("i", f"iD{j}", RIp.at[zb, yj, hi], RZ.at[5, j], zm)

    def in_y(j):
        got(f"iD{j}", RZ.at[pl.ds(2, 4), j])
        yj = (y + j) % 4
        first = RIf[zh, yj, lo] + RZ[4, j].astype(f32) + RZ[3, j].astype(f32)
        second = RIf[zh, yj, hi] + RZ[2, j].astype(f32) + RZ[5, j].astype(f32)
        if j == 0:
            JYf[lo] = first
            JYf[hi] = second
        else:
            JYb[j, lo] = first.astype(bf16)
            JYb[j, hi] = second.astype(bf16)
            send("iy", "iy", JYb.at[j], RY.at[j - 1], (yp, y2, ym)[j - 1])

    def in_final():
        got("iy", RY)
        total = JYf[...]
        for i in range(3):
            total += RY[i].astype(f32)
        RI[0, 0, k] = total.astype(bf16)

    xn, xb, xo = (x + 1) % 4, (x + 3) % 4, (x + 2) % 4

    def out_partial(q, n):
        n0, n1 = ((0, 512), (512, 896))[n]
        total = jnp.dot(G[q].reshape(256, 3584), B[:, n0:n1], preferred_element_type=f32)
        total = total.reshape(4, 2, 32, n1 - n0)
        Pf[q, :, :, :, n0:n1] = total
        Pb[q, :, :, :, n0:n1] = total.astype(bf16)
        if n == 1:
            send("x", f"A+{q}", Pb.at[q, xo, 0], RX.at[q, 0], xp)
            send("x", f"A-{q}", Pb.at[q, xo, 1], RX.at[q, 1], xm)
            send("x", f"D{q}", Pb.at[q, xn, 1], RX.at[q, 2], xp)
            send("x", f"D{q}", Pb.at[q, xb, 0], RX.at[q, 3], xm)

    def out_add(way, q):
        got(f"A{way}{q}", RX.at[q, 0 if way == "+" else 1])
        if way == "+":
            Pb[q, xn, 0] = (Pf[q, xn, 0] + RX[q, 0].astype(f32)).astype(bf16)
            send("x", f"D{q}", Pb.at[q, xn, 0], RX.at[q, 4], xp)
        else:
            Pb[q, xb, 1] = (Pf[q, xb, 1] + RX[q, 1].astype(f32)).astype(bf16)
            send("x", f"D{q}", Pb.at[q, xb, 1], RX.at[q, 5], xm)

    def out_x(q):
        got(f"D{q}", RX.at[q, pl.ds(2, 4)])
        Pf[q, x, 0] = Pf[q, x, 0] + RX[q, 4].astype(f32) + RX[q, 3].astype(f32)
        Pf[q, x, 1] = Pf[q, x, 1] + RX[q, 2].astype(f32) + RX[q, 5].astype(f32)
        SB[q] = Pf[q, x, 1 - zl].astype(bf16)
        send("o", f"zl{q}", SB.at[q], SZ.at[q], zlp)

    def out_zl(q):
        got(f"zl{q}", SZ.at[q])
        RO[q, x, zl] = (Pf[q, x, zl] + SZ[q].astype(f32)).astype(bf16)
        mine = RO.at[q, x, zl]
        send("o", f"oz{q}", mine, mine, zlp)
        send("o", f"op{q}", mine, mine, xp)
        send("o", f"o{q}", mine, mine, xm)

    def out_pair(q):
        other = RO.at[q, x, 1 - zl]
        got(f"oz{q}", other)
        send("o", f"o{q}", other, other, xp)
        send("o", f"omz{q}", other, other, xm)

    def out_far(way, q):
        if way == "+":
            src = RO.at[q, xb, zl]
            got(f"op{q}", src)
            send("o", f"o{q}", src, src, xp)
        else:
            src = RO.at[q, xn, 1 - zl]
            got(f"omz{q}", src)
            send("o", f"o{q}", src, src, xm)

    def rotated(q):
        got(f"o{q}", RO.at[q, pl.ds(0, 2)])
        gather_done("r", RI, q)

    def product(left, right):
        return lax.dot_general(left, right, (((0,), (0,)), ((), ())), preferred_element_type=f32)

    outs = []

    def coeffs(q):
        if q == 0:
            rotated(0)
            rotated(1)
            ACC[...] = product(RO[0:2].reshape(512, 896), RI[0:2].reshape(512, 1024))
        elif q == 2:
            rotated(2)
            ACC[...] += product(RO[2].reshape(256, 896), RI[2].reshape(256, 1024))
        else:
            rotated(3)
            loads["eig"].wait()
            right = RI[3].reshape(256, 1024)
            for i, (m, n) in enumerate(((0, 256), (256, 512), (512, 768), (768, 896))):
                total = ACC[m:n] + product(RO[3, :, :, :, m:n].reshape(256, n - m), right)
                OUT[m:n] = (total / 1024 / (EIG[m:n].astype(f32) + damping)).astype(bf16)
                cp = pltpu.make_async_copy(OUT.at[pl.ds(m, n - m)], out.at[pl.ds(m, n - m)], lsem.at[len(loads) + i])
                cp.start()
                outs.append(cp)

    def drain():
        for t, buf in (("g", G), ("r", RI)):
            all_sent(t + "z", buf.at[pl.ds(0, 3), 0, 0])
            all_sent(t + "y", buf.at[pl.ds(0, 3), :, 0])
            all_sent(t + "s", buf.at[pl.ds(0, 2)])
        for group, ref in (("ibi", IB.at[k]), ("iq", QI.at[k]), ("i", RZ), ("iy", RY), ("x", RX), ("o", RO)):
            all_sent(group, ref)
        for cp in outs:
            cp.wait()

    gather_start("g", G, g_in)
    in_start()
    in_partial()
    gather_y("g", G, 3, 0, 0)
    gather_y("g", G, 1, 0, 1)
    gather_y("g", G, 1, 0, 0)
    gather_y("g", G, 3, 0, 1)
    in_near(0)
    gather_z("g", G, 1)
    gather_far("g", G, 0)
    loads["g"].wait()
    loads["bo"].wait()
    gather_done("g", G, 0)
    out_partial(0, 0)
    gather_y("g", G, 3, 1, 0)
    gather_y("g", G, 1, 1, 1)
    out_partial(0, 1)
    gather_z("g", G, 2)
    in_far(0)
    in_far(1)
    gather_y("g", G, 1, 1, 0)
    gather_y("g", G, 3, 1, 1)
    in_far(2)
    out_add("+", 0)
    out_add("-", 0)
    gather_far("g", G, 1)
    in_far(3)
    in_near(1)
    gather_done("g", G, 1)
    out_partial(1, 0)
    gather_y("g", G, 3, 2, 0)
    gather_y("g", G, 1, 2, 1)
    in_add("+", 0)
    in_add("-", 0)
    gather_z("g", G, 3)
    out_x(0)
    out_partial(1, 1)
    gather_y("g", G, 1, 2, 0)
    gather_y("g", G, 3, 2, 1)
    in_add("+", 1)
    in_add("-", 1)
    in_add("+", 2)
    in_add("-", 2)
    in_add("+", 3)
    gather_far("g", G, 2)
    in_add("-", 3)
    out_add("+", 1)
    out_add("-", 1)
    in_near(2)
    gather_done("g", G, 2)
    out_partial(2, 0)
    in_y(0)
    gather_y("g", G, 3, 3, 0)
    gather_y("g", G, 1, 3, 1)
    in_near(3)
    out_zl(0)
    out_x(1)
    out_partial(2, 1)
    gather_y("g", G, 1, 3, 0)
    gather_y("g", G, 3, 3, 1)
    in_y(1)
    out_far("+", 0)
    gather_far("g", G, 3)
    out_add("+", 2)
    out_add("-", 2)
    in_y(2)
    gather_done("g", G, 3)
    out_partial(3, 0)
    in_y(3)
    out_pair(0)
    out_partial(3, 1)
    out_zl(1)
    out_x(2)
    out_far("-", 0)
    in_final()
    gather_start("r", RI, RI.at[0, 0, k])
    out_add("+", 3)
    out_pair(1)
    out_add("-", 3)
    out_zl(2)
    gather_y("r", RI, 1, 0, 1)
    gather_y("r", RI, 3, 0, 0)
    gather_y("r", RI, 1, 0, 0)
    gather_y("r", RI, 3, 0, 1)
    out_far("+", 1)
    gather_z("r", RI, 1)
    gather_far("r", RI, 0)
    out_far("-", 1)
    out_pair(2)
    gather_z("r", RI, 2)
    gather_y("r", RI, 1, 1, 1)
    gather_y("r", RI, 3, 1, 0)
    out_far("+", 2)
    out_x(3)
    gather_y("r", RI, 1, 1, 0)
    gather_y("r", RI, 3, 1, 1)
    gather_y("r", RI, 1, 2, 1)
    gather_y("r", RI, 3, 2, 0)
    gather_z("r", RI, 3)
    gather_y("r", RI, 1, 2, 0)
    gather_y("r", RI, 3, 2, 1)
    gather_far("r", RI, 1)
    out_zl(3)
    out_far("-", 2)
    gather_far("r", RI, 2)
    gather_y("r", RI, 1, 3, 1)
    gather_y("r", RI, 3, 3, 0)
    coeffs(0)
    gather_y("r", RI, 1, 3, 0)
    gather_y("r", RI, 3, 3, 1)
    out_pair(3)
    out_far("+", 3)
    gather_far("r", RI, 3)
    coeffs(2)
    out_far("-", 3)
    coeffs(3)
    drain()
    assert (len(sent), len(arrived)) == (SENT, ARRIVED), (len(sent), len(arrived))


def shards(query_grads, query_inputs, out_basis, in_basis, eig_grid):
    bf16, f32, vmem = jnp.bfloat16, jnp.float32, pltpu.VMEM
    any_space = pl.BlockSpec(memory_space=pl.ANY)
    return pl.pallas_call(
        kernel,
        out_shape=jax.ShapeDtypeStruct((896, 1024), bf16),
        in_specs=[any_space] * 5,
        out_specs=any_space,
        scratch_shapes=[
            vmem((4, 4, 2, 32, 3584), bf16),
            vmem((3584, 896), bf16),
            vmem((2, 4, 4, 32, 256), bf16),
            vmem((2, 256, 1024), bf16),
            vmem((4, 4, 32, 1024), bf16),
            vmem((4, 4, 32, 1024), f32),
            vmem((6, 4, 16, 1024), bf16),
            vmem((4, 32, 1024), bf16),
            vmem((32, 1024), f32),
            vmem((3, 32, 1024), bf16),
            vmem((4, 4, 2, 32, 1024), bf16),
            vmem((4, 4, 2, 32, 896), bf16),
            vmem((4, 4, 2, 32, 896), f32),
            vmem((4, 6, 32, 896), bf16),
            vmem((4, 32, 896), bf16),
            vmem((4, 32, 896), bf16),
            vmem((4, 4, 2, 32, 896), bf16),
            vmem((896, 1024), f32),
            vmem((896, 1024), bf16),
            vmem((896, 1024), bf16),
            pltpu.SemaphoreType.DMA((SENT,)),
            pltpu.SemaphoreType.DMA((ARRIVED,)),
            pltpu.SemaphoreType.DMA((9,)),
        ],
        compiler_params=pltpu.CompilerParams(
            collective_id=0, has_side_effects=True, vmem_limit_bytes=56 * 2**20
        ),
        cost_estimate=pl.CostEstimate(flops=9_000_000_000, bytes_accessed=12_000_000, transcendentals=0),
        name="precondition",
    )(query_grads, query_inputs.reshape(4, 4, 2, 32, 256), out_basis, in_basis, eig_grid)


def solution(mesh):
    return jax.shard_map(
        shards,
        mesh=mesh,
        in_specs=(
            P("col", "row"),
            P(None, "col"),
            P("row", "col"),
            P("col", "row"),
            P("col", "row"),
        ),
        out_specs=P("col", "row"),
        check_vma=False,
    )
```

time: 389 us -> 82.2 us (0.21)
  blocking collectives: 352 us -> 0 us
  Pallas kernels: 0 us -> 79.2 us
  matrix products: 22.6 us -> 0 us
  between operations: 13.4 us -> 0.01 us
    psum x2 -> x0, blocking collectives: 352 us -> none  [the longest x1 211 us: shards(): rotated_in = lax.psum(in_partial, 'col').astype(jnp.bfloat16)]
    pallas_call x0 -> x1, Pallas kernels: none -> 79.2 us  [shards(): pl.pallas_call(kernel, out_shape=jax.ShapeDtypeStruct((896, 1024), bf16),...]
    dot_general x3 -> x0, matrix products: 22.6 us -> none  [the longest x1 13.1 us: shards(): jnp.dot(lax.all_gather(query_grads, 'col', axis=0, tiled=True), out_basis...]
  transfers between devices with their start and end apart: 1 -> 0, of which waited for: 0 -> 0; matrix products, arithmetic and copies ran while one was open for 1% -> 0% of each run, Pallas kernels for 0% -> 0%
where the time goes in v2:
time: 82.2 us; the launch traced here: 82.1 us
  Pallas kernels  79.2 us (96%)
  local copies, waits for them, and re-layouts  2.87 us (3%)
    pallas_call x1, Pallas kernels, shards(): pl.pallas_call(kernel, out_shape=jax.ShapeDtypeStruct((896, 1024), bf16),...  79.2 us
    unnamed x1, local copies, waits for them, and re-layouts  2.87 us

profile of v2, /device:TPU:2, one launch (start us, length us, event | category | flops | bytes accessed | tf_op | source)
XLA Modules:
  0.0 82.1 jit_solution(16280566174532810744)
XLA Ops:
  0.0 79.2 %precondition.1 = bf16[896,1024]{1,0:T(8,128)(2,1)} custom-call(bf16[32,3584]{1,0:T(8,128)(2,1)} %g_in.1, bf16[4,4,2,32,256]{4,3,2,1,0:T(8,128)(2,1)} %bitcast.1, bf16[3584,896]{1,0:T(8,128)(2,1)} %bo_in.1, bf16[256,1024]{1,0:T(8,128)(2,1)} %bi_in.1, bf16[896,1024]{1,0:T(8,128)(2,1)} %eig_in.1), custom_call_target="tpu_custom_call" | custom-call | flops 8999999488 | bytes 12000000 | tf_op jit(solution)/shard_map/precondition/pallas_call | solution.py:386
  79.2 2.9 %copy.7 = bf16[896,1024]{1,0:T(8,128)(2,1)} copy(bf16[896,1024]{1,0:T(8,128)(2,1)} %precondition.1) | data formatting | bytes 3670016

commit v3 on v2

--- a/solution.py
+++ b/solution.py
@@ -288,10 +288,10 @@
     gather_far("g", G, 1)
     in_far(3)
     in_near(1)
+    gather_y("g", G, 3, 2, 0)
+    gather_y("g", G, 1, 2, 1)
     gather_done("g", G, 1)
     out_partial(1, 0)
-    gather_y("g", G, 3, 2, 0)
-    gather_y("g", G, 1, 2, 1)
     in_add("+", 0)
     in_add("-", 0)
     gather_z("g", G, 3)
@@ -309,12 +309,12 @@
     out_add("+", 1)
     out_add("-", 1)
     in_near(2)
+    in_near(3)
+    gather_y("g", G, 3, 3, 0)
+    gather_y("g", G, 1, 3, 1)
     gather_done("g", G, 2)
     out_partial(2, 0)
     in_y(0)
-    gather_y("g", G, 3, 3, 0)
-    gather_y("g", G, 1, 3, 1)
-    in_near(3)
     out_zl(0)
     out_x(1)
     out_partial(2, 1)
@@ -322,14 +322,14 @@
     gather_y("g", G, 3, 3, 1)
     in_y(1)
     out_far("+", 0)
+    out_pair(0)
     gather_far("g", G, 3)
     out_add("+", 2)
     out_add("-", 2)
     in_y(2)
+    in_y(3)
     gather_done("g", G, 3)
     out_partial(3, 0)
-    in_y(3)
-    out_pair(0)
     out_partial(3, 1)
     out_zl(1)
     out_x(2)
@@ -346,35 +346,35 @@
     gather_y("r", RI, 3, 0, 1)
     out_far("+", 1)
     gather_z("r", RI, 1)
-    gather_far("r", RI, 0)
     out_far("-", 1)
     out_pair(2)
+    out_x(3)
+    gather_far("r", RI, 0)
     gather_z("r", RI, 2)
     gather_y("r", RI, 1, 1, 1)
     gather_y("r", RI, 3, 1, 0)
     out_far("+", 2)
-    out_x(3)
     gather_y("r", RI, 1, 1, 0)
     gather_y("r", RI, 3, 1, 1)
+    out_zl(3)
     gather_y("r", RI, 1, 2, 1)
     gather_y("r", RI, 3, 2, 0)
     gather_z("r", RI, 3)
     gather_y("r", RI, 1, 2, 0)
     gather_y("r", RI, 3, 2, 1)
     gather_far("r", RI, 1)
-    out_zl(3)
+    out_pair(3)
+    out_far("+", 3)
     out_far("-", 2)
     gather_far("r", RI, 2)
     gather_y("r", RI, 1, 3, 1)
     gather_y("r", RI, 3, 3, 0)
     coeffs(0)
+    out_far("-", 3)
     gather_y("r", RI, 1, 3, 0)
     gather_y("r", RI, 3, 3, 1)
-    out_pair(3)
-    out_far("+", 3)
     gather_far("r", RI, 3)
     coeffs(2)
-    out_far("-", 3)
     coeffs(3)
     drain()
     assert (len(sent), len(arrived)) == (SENT, ARRIVED), (len(sent), len(arrived))

time: 82.2 us -> 78.2 us (0.951)
  Pallas kernels: 79.2 us -> 74.7 us
    pallas_call x1, Pallas kernels: 79.2 us -> 74.7 us  [shards(): pl.pallas_call(kernel, out_shape=jax.ShapeDtypeStruct((896, 1024), bf16),...]
where the time goes in v3:
time: 78.2 us; the launch traced here: 77.6 us
  Pallas kernels  74.7 us (96%)
  local copies, waits for them, and re-layouts  2.87 us (4%)
    pallas_call x1, Pallas kernels, shards(): pl.pallas_call(kernel, out_shape=jax.ShapeDtypeStruct((896, 1024), bf16),...  74.7 us
    unnamed x1, local copies, waits for them, and re-layouts  2.87 us

profile of v3, /device:TPU:2, one launch (start us, length us, event | category | flops | bytes accessed | tf_op | source)
XLA Modules:
  0.0 77.6 jit_solution(11251895343861769719)
XLA Ops:
  0.0 74.7 %precondition.1 = bf16[896,1024]{1,0:T(8,128)(2,1)} custom-call(bf16[32,3584]{1,0:T(8,128)(2,1)} %g_in.1, bf16[4,4,2,32,256]{4,3,2,1,0:T(8,128)(2,1)} %bitcast.1, bf16[3584,896]{1,0:T(8,128)(2,1)} %bo_in.1, bf16[256,1024]{1,0:T(8,128)(2,1)} %bi_in.1, bf16[896,1024]{1,0:T(8,128)(2,1)} %eig_in.1), custom_call_target="tpu_custom_call" | custom-call | flops 8999999488 | bytes 12000000 | tf_op jit(solution)/shard_map/precondition/pallas_call | solution.py:386
  74.7 2.9 %copy.7 = bf16[896,1024]{1,0:T(8,128)(2,1)} copy(bf16[896,1024]{1,0:T(8,128)(2,1)} %precondition.1) | data formatting | bytes 3670016

commit v4 on v3

--- a/solution.py
+++ b/solution.py
@@ -11,7 +11,7 @@
 
 
 def kernel(g_in, q_in, bo_in, bi_in, eig_in, out, G, B, QI, IB, RIp, RIf, RZ, JYb, JYf, RY, RI,
-           Pb, Pf, RX, SB, SZ, RO, ACC, EIG, OUT, ssem, rsem, lsem):
+           Pb, Pf, RX, SB, SZ, RO, ACC, EIG, SCALE, OUT, ssem, rsem, lsem):
     f32, bf16 = jnp.float32, jnp.bfloat16
     r, c = lax.axis_index("row"), lax.axis_index("col")
     x, zl = r // 2, r % 2
@@ -241,14 +241,17 @@
             ACC[...] += product(RO[2].reshape(256, 896), RI[2].reshape(256, 1024))
         else:
             rotated(3)
-            loads["eig"].wait()
             right = RI[3].reshape(256, 1024)
             for i, (m, n) in enumerate(((0, 256), (256, 512), (512, 768), (768, 896))):
                 total = ACC[m:n] + product(RO[3, :, :, :, m:n].reshape(256, n - m), right)
-                OUT[m:n] = (total / 1024 / (EIG[m:n].astype(f32) + damping)).astype(bf16)
+                OUT[m:n] = (total * SCALE[m:n]).astype(bf16)
                 cp = pltpu.make_async_copy(OUT.at[pl.ds(m, n - m)], out.at[pl.ds(m, n - m)], lsem.at[len(loads) + i])
                 cp.start()
                 outs.append(cp)
+
+    def scale():
+        loads["eig"].wait()
+        SCALE[...] = 1.0 / (1024 * (EIG[...].astype(f32) + damping))
 
     def drain():
         for t, buf in (("g", G), ("r", RI)):
@@ -283,6 +286,7 @@
     gather_y("g", G, 1, 1, 0)
     gather_y("g", G, 3, 1, 1)
     in_far(2)
+    scale()
     out_add("+", 0)
     out_add("-", 0)
     gather_far("g", G, 1)
@@ -408,6 +412,7 @@
             vmem((4, 4, 2, 32, 896), bf16),
             vmem((896, 1024), f32),
             vmem((896, 1024), bf16),
+            vmem((896, 1024), f32),
             vmem((896, 1024), bf16),
             pltpu.SemaphoreType.DMA((SENT,)),
             pltpu.SemaphoreType.DMA((ARRIVED,)),

time: 78.2 us -> 77.9 us (level)
  no operation moved by 1% of the time
where the time goes in v4:
time: 77.9 us; the launch traced here: 77.4 us
  Pallas kernels  74.5 us (96%)
  local copies, waits for them, and re-layouts  2.87 us (4%)
    pallas_call x1, Pallas kernels, shards(): pl.pallas_call(kernel, out_shape=jax.ShapeDtypeStruct((896, 1024), bf16),...  74.5 us
    unnamed x1, local copies, waits for them, and re-layouts  2.87 us

profile of v4, /device:TPU:2, one launch (start us, length us, event | category | flops | bytes accessed | tf_op | source)
XLA Modules:
  0.0 77.4 jit_solution(1533459344294223470)
XLA Ops:
  0.0 74.5 %precondition.1 = bf16[896,1024]{1,0:T(8,128)(2,1)} custom-call(bf16[32,3584]{1,0:T(8,128)(2,1)} %g_in.1, bf16[4,4,2,32,256]{4,3,2,1,0:T(8,128)(2,1)} %bitcast.1, bf16[3584,896]{1,0:T(8,128)(2,1)} %bo_in.1, bf16[256,1024]{1,0:T(8,128)(2,1)} %bi_in.1, bf16[896,1024]{1,0:T(8,128)(2,1)} %eig_in.1), custom_call_target="tpu_custom_call" | custom-call | flops 8999999488 | bytes 12000000 | tf_op jit(solution)/shard_map/precondition/pallas_call | solution.py:390
  74.5 2.9 %copy.7 = bf16[896,1024]{1,0:T(8,128)(2,1)} copy(bf16[896,1024]{1,0:T(8,128)(2,1)} %precondition.1) | data formatting | bytes 3670016
